TPU v7x, 256 devices: a whole 4x4x8 slice. The times are simulated.
256 devices in a mesh: row: 32 (over x, y, core), col: 8 (over z).
Axes of the slice: x: 4, y: 4, z: 8, core: 2. Of those that a mesh axis runs over, the one named last changes fastest.
Arguments:
- source: bfloat16 [32768, 128], P(('row', 'col')), may hold values from -10 to 10
- target: bfloat16 [32768, 128], P(('col', 'row')), may hold values from -80 to 80
- target_potential: bfloat16 [32768], P(('col', 'row')), may hold values from -4 to 4
- prev_moment: float32 [128, 128], replicated, may hold values from -0.1 to 0.5
Outputs:
- moment: float32 [128, 128], replicated
- source_potential: float32 [32768], P('row')
- target_update: float32 [32768], P(('col', 'row'))
All inputs are finite; a program needn't handle non-finite values.
Results may differ from a plain program's by a relative error of at most 0.0059.
Values may be sent and summed in bfloat16 or wider, within the bound.
A program may use at most 64 MiB of HBM per device.

v0:
```python
import math
import jax
import jax.numpy as jnp
from jax import lax
from jax.sharding import PartitionSpec as P

ITERS = 2


def project(rows_block, matrix):
    return jnp.dot(rows_block.astype(jnp.float32), matrix, precision=lax.Precision.HIGHEST).astype(
        jnp.bfloat16
    )


def tile_costs(projected, cols_block):
    return -4.0 * lax.dot_general(
        projected, cols_block, (((1,), (1,)), ((), ())), preferred_element_type=jnp.float32
    )


def row_totals(scores):
    top_score = lax.pmax(jnp.max(scores, axis=1), "col")
    mass_total = lax.psum(jnp.sum(jnp.exp(scores - top_score[:, None]), axis=1), "col")
    return top_score + jnp.log(mass_total)


def column_totals(scores):
    top_score = lax.pmax(jnp.max(scores, axis=0), "row")
    mass_total = lax.psum(jnp.sum(jnp.exp(scores - top_score[None, :]), axis=0), "row")
    return top_score + jnp.log(mass_total)


def per_device(source, target, target_potential, prev_moment):
    rows_block = lax.all_gather(source, "col", axis=0, tiled=True)
    cols_block, potential = (
        lax.all_gather(target, "row", axis=0, tiled=True),
        lax.all_gather(target_potential, "row", axis=0, tiled=True),
    )
    row_devices = lax.axis_size("row")
    rows_total = rows_block.shape[0] * row_devices
    cols_total = cols_block.shape[0] * lax.axis_size("col")
    share_width = cols_block.shape[0] // row_devices
    position = lax.axis_index("row")
    column = potential.astype(jnp.float32)
    scores = column[None, :] - tile_costs(project(rows_block, prev_moment), cols_block)
    spread = row_totals(scores)
    weights = (jnp.exp(scores - spread[:, None]) / rows_total).astype(jnp.bfloat16)
    carried = jnp.dot(weights, cols_block, preferred_element_type=jnp.float32)
    partial_moment = lax.dot_general(
        rows_block.astype(jnp.float32),
        carried,
        (((0,), (0,)), ((), ())),
        precision=lax.Precision.HIGHEST,
    )
    moment = lax.psum(partial_moment, ("row", "col"))
    cost_tile = tile_costs(project(rows_block, moment), cols_block)
    source_potential = jnp.zeros((rows_block.shape[0],), jnp.float32)
    own_share = jnp.zeros((share_width,), jnp.float32)
    for iteration in range(ITERS):
        source_potential = math.log(cols_total) - row_totals(column[None, :] - cost_tile)
        column_scores = source_potential[:, None] - cost_tile
        column = math.log(rows_total) - column_totals(column_scores)
        own_share = lax.dynamic_slice_in_dim(column, position * share_width, share_width)
    return (moment, source_potential, own_share)


def solution(mesh):
    placed = (P(("row", "col"), None), P(("col", "row"), None), P(("col", "row")), P())
    return jax.shard_map(
        per_device,
        mesh=mesh,
        in_specs=placed,
        out_specs=(P(), P("row"), P(("col", "row"))),
        check_vma=False,
    )
```

profile of v0, /device:TPU:32, one launch (start us, length us, event | category | flops | bytes accessed | tf_op | source)
XLA Modules:
  0.0 979.2 jit_solution(412638877074749381)
XLA Ops:
  7.2 0.0 copy-start
  7.2 0.0 all-gather.3.cloned.1.call-start
  7.2 0.7 all-gather.3.cloned.1.call-update
  7.9 0.0 all-reduce.2.cloned.1.call-start
  8.0 21.8 %all-gather = bf16[32,1,128]{2,1,0:T(2,128)(2,1)S(1)} all-gather(bf16[1,1,128]{2,1,0:T(2,128)(2,1)} %bitcast.20), channel_id=1, replica_groups=mesh['row'=32,'col'=8] {'row'}, dimensions={0}, use_global_device_ids=true | all-gather | bytes 8448 | tf_op jit(solution)/shard_map/all_gather | solution.py:38
  29.8 27.7 %all_gather.10 = bf16[1024,128]{1,0:T(8,128)(2,1)S(1)} all-gather(bf16[128,128]{1,0:T(8,128)(2,1)} %param.4), channel_id=1, replica_groups=mesh['row'=32,'col'=8] {'col'}, dimensions={0}, use_global_device_ids=true | all-gather | bytes 294912 | tf_op jit(solution)/shard_map/all_gather | solution.py:35
  57.5 0.0 copy-done
  57.5 0.4 convolution_convert_fusion.1
  57.9 3.1 all-gather.3.cloned.1.call-done
  61.0 0.0 copy-start.1
  61.0 8.3 fusion
  69.3 16.0 %pmax.35 = f32[1024]{0:T(1024)S(1)} all-reduce(f32[1024]{0:T(1024)S(1)} %get-tuple-element.9), channel_id=1, replica_groups=mesh['row'=32,'col'=8] {'col'}, use_global_device_ids=true, to_apply=%region_1.0 | all-reduce | flops 1024 | bytes 8192 | tf_op jit(solution)/shard_map/pmax | solution.py:23
  85.4 7.8 exponential_reduce_fusion.4
  93.2 16.0 %psum.42 = f32[1024]{0:T(1024)S(1)} all-reduce(f32[1024]{0:T(1024)S(1)} %exponential_reduce_fusion.4), channel_id=1, replica_groups=mesh['row'=32,'col'=8] {'col'}, use_global_device_ids=true, to_apply=%region_3.0 | all-reduce | flops 1024 | bytes 8192 | tf_op jit(solution)/shard_map/psum | solution.py:24
  109.2 0.0 copy-done.1
  109.2 7.8 fusion.1
  117.0 1.2 convolution_bitcast_fusion
  118.2 0.0 all-reduce.2.cloned.1.call-update
  118.3 234.4 %all-reduce.2.cloned.1.call-done = f32[128,128]{0,1:T(8,128)} async-done(((f32[128,128]{0,1:T(8,128)}), f32[128,128]{0,1:T(8,128)}) %all-reduce.2.cloned.1.call-update) | async-done | bytes 65552 | tf_op jit(solution)/shard_map/psum | solution.py:56
  352.7 1.2 convolution_convert_fusion
  353.9 7.0 subtract_reduce_fusion.3
  360.9 15.2 %pmax.36 = f32[1024]{0:T(1024)S(1)} all-reduce(f32[1024]{0:T(1024)S(1)} %get-tuple-element.11), channel_id=1, replica_groups=mesh['row'=32,'col'=8] {'col'}, use_global_device_ids=true, to_apply=%region_6.0 | all-reduce | flops 1024 | bytes 8192 | tf_op jit(solution)/shard_map/pmax | solution.py:23
  376.1 7.8 exponential_reduce_fusion.3
  384.0 15.1 %psum.44 = f32[1024]{0:T(1024)S(1)} all-reduce(f32[1024]{0:T(1024)S(1)} %exponential_reduce_fusion.3), channel_id=1, replica_groups=mesh['row'=32,'col'=8] {'col'}, use_global_device_ids=true, to_apply=%region_8.0 | all-reduce | flops 1024 | bytes 8192 | tf_op jit(solution)/shard_map/psum | solution.py:24
  399.1 7.7 subtract_reduce_fusion.2
  406.8 124.0 %pmax.37 = f32[4096]{0:T(1024)S(1)} all-reduce(f32[4096]{0:T(1024)S(1)} %subtract_reduce_fusion.2), channel_id=1, replica_groups=mesh['row'=32,'col'=8] {'row'}, use_global_device_ids=true, to_apply=%region_10.0 | all-reduce | flops 4096 | bytes 32768 | tf_op jit(solution)/shard_map/pmax | solution.py:29
  530.8 7.7 exponential_reduce_fusion.2
  538.5 123.8 %psum.45 = f32[4096]{0:T(1024)S(1)} all-reduce(f32[4096]{0:T(1024)S(1)} %exponential_reduce_fusion.2), channel_id=1, replica_groups=mesh['row'=32,'col'=8] {'row'}, use_global_device_ids=true, to_apply=%region_12.0 | all-reduce | flops 4096 | bytes 32768 | tf_op jit(solution)/shard_map/psum | solution.py:30
  662.3 7.5 subtract_reduce_fusion.1
  669.8 15.2 %pmax.38 = f32[1024]{0:T(1024)S(1)} all-reduce(f32[1024]{0:T(1024)S(1)} %subtract_reduce_fusion.1), channel_id=1, replica_groups=mesh['row'=32,'col'=8] {'col'}, use_global_device_ids=true, to_apply=%region_14.0 | all-reduce | flops 1024 | bytes 8192 | tf_op jit(solution)/shard_map/pmax | solution.py:23
  685.0 7.8 exponential_reduce_fusion.1
  692.8 15.1 %psum.46 = f32[1024]{0:T(1024)S(1)} all-reduce(f32[1024]{0:T(1024)S(1)} %exponential_reduce_fusion.1), channel_id=1, replica_groups=mesh['row'=32,'col'=8] {'col'}, use_global_device_ids=true, to_apply=%region_16.0 | all-reduce | flops 1024 | bytes 8192 | tf_op jit(solution)/shard_map/psum | solution.py:24
  708.0 0.0 copy-start.3
  708.0 0.0 copy-start.2
  708.0 7.8 subtract_reduce_fusion
  715.7 123.8 %pmax.39 = f32[4096]{0:T(1024)S(1)} all-reduce(f32[4096]{0:T(1024)S(1)} %subtract_reduce_fusion), channel_id=1, replica_groups=mesh['row'=32,'col'=8] {'row'}, use_global_device_ids=true, to_apply=%region_18.0 | all-reduce | flops 4096 | bytes 32768 | tf_op jit(solution)/shard_map/pmax | solution.py:29
  839.5 7.7 exponential_reduce_fusion
  847.3 0.0 copy-done.3
  847.3 123.8 %psum.47 = f32[4096]{0:T(1024)S(1)} all-reduce(f32[4096]{0:T(1024)S(1)} %exponential_reduce_fusion), channel_id=1, replica_groups=mesh['row'=32,'col'=8] {'row'}, use_global_device_ids=true, to_apply=%region_20.0 | all-reduce | flops 4096 | bytes 32768 | tf_op jit(solution)/shard_map/psum | solution.py:30
  971.0 0.6 fusion.2
  971.6 0.0 copy-done.2
  971.6 0.7 copy.8
  (5 shorter events, 0.1 us)
Async XLA Ops:
  7.2 50.3 %copy-start = (f32[128,128]{1,0:T(8,128)S(1)}, f32[128,128]{1,0:T(8,128)}, u32[]{:S(2)}) copy-start(f32[128,128]{1,0:T(8,128)} %param.7) | copy-start | bytes 196612
  7.2 53.8 %all-gather.3.cloned.1.call-start = ((), (), s32[]{:S(2)}) async-start(), calls=%async_computation | async-start | bytes 1081344 | tf_op jit(solution)/shard_map/all_gather | solution.py:37
  7.9 344.7 %all-reduce.2.cloned.1.call-start = ((), (), s32[]{:S(2)}) async-start(), calls=%async_computation.1 | async-start | bytes 131072 | tf_op jit(solution)/shard_map/psum | solution.py:56
  61.0 48.2 %copy-start.1 = (bf16[4096,128]{1,0:T(8,128)(2,1)S(1)}, bf16[4096,128]{1,0:T(8,128)(2,1)}, u32[]{:S(2)}) copy-start(bf16[4096,128]{1,0:T(8,128)(2,1)} %all-gather.3.cloned.1.call-done) | copy-start | bytes 3145732
  708.0 139.3 %copy-start.3 = (f32[1024]{0:T(1024)}, f32[1024]{0:T(1024)S(1)}, u32[]{:S(2)}) copy-start(f32[1024]{0:T(1024)S(1)} %add_subtract_fusion.1) | copy-start | bytes 12292
  708.0 263.7 %copy-start.2 = (f32[128,128]{0,1:T(8,128)S(1)}, f32[128,128]{0,1:T(8,128)}, u32[]{:S(2)}) copy-start(f32[128,128]{0,1:T(8,128)} %all-reduce.2.cloned.1.call-done) | copy-start | bytes 196612
Sparse Core Ops, SparseCore 0:
  10.6 50.3 all-gather.2
  118.4 234.2 all-reduce.1
where the time goes:
time: 980 us; the launch traced here: 979 us
  blocking collectives  638 us (65%)
  waiting for transfers between devices  238 us (24%)
  other arithmetic  62.6 us (6%)
  matrix products  25.9 us (3%)
  between operations  14.1 us (1%)
    pmax x2, blocking collectives, column_totals(): top_score = lax.pmax(jnp.max(scores, axis=0), 'row')  248 us
    psum x2, blocking collectives, column_totals(): lax.psum(jnp.sum(jnp.exp(scores - top_score[None, :]), axis=0), 'row')  248 us
    psum x1, waiting for transfers between devices, per_device(): moment = lax.psum(partial_moment, ('row', 'col'))  234 us
    pmax x3, blocking collectives, row_totals(): top_score = lax.pmax(jnp.max(scores, axis=1), 'col')  46.5 us
    psum x3, blocking collectives, row_totals(): lax.psum(jnp.sum(jnp.exp(scores - top_score[:, None]), axis=1), 'col')  46.2 us
    all_gather x1, blocking collectives, per_device(): rows_block = lax.all_gather(source, 'col', axis=0, tiled=True)  27.7 us
    reduce_sum x3, other arithmetic, row_totals(): jnp.sum(jnp.exp(scores - top_score[:, None]), axis=1)  23.5 us
    all_gather x1, blocking collectives, per_device(): lax.all_gather(target_potential, 'row', axis=0, tiled=True)  21.8 us
  transfers between devices with their start and end apart: 2, of which 2 were waited for; matrix products, arithmetic and copies ran while one was open for 0% of the time, Pallas kernels for 0%

commit v1 on v0

--- a/solution.py
+++ b/solution.py
@@ -27,7 +27,9 @@
 
 def column_totals(scores):
     top_score = lax.pmax(jnp.max(scores, axis=0), "row")
-    mass_total = lax.psum(jnp.sum(jnp.exp(scores - top_score[None, :]), axis=0), "row")
+    mass_total = jnp.sum(
+        lax.all_gather(jnp.sum(jnp.exp(scores - top_score[None, :]), axis=0), "row"), axis=0
+    )
     return top_score + jnp.log(mass_total)
 
 

time: 980 us -> 778 us (0.79)
  blocking collectives: 638 us -> 433 us
    psum x2 -> x0, blocking collectives: 248 us -> none  [column_totals(): lax.psum(jnp.sum(jnp.exp(scores - top_score[None, :]), axis=0), 'row')]
    all_gather x0 -> x2, blocking collectives: none -> 43.5 us  [column_totals(): lax.all_gather(jnp.sum(jnp.exp(scores - top_score[None, :]), axis=0), 'row')]
where the time goes in v1:
time: 778 us; the launch traced here: 776 us
  blocking collectives  433 us (56%)
  waiting for transfers between devices  238 us (31%)
  other arithmetic  62.7 us (8%)
  matrix products  25.9 us (3%)
  between operations  14.2 us (2%)
    pmax x2, blocking collectives, column_totals(): top_score = lax.pmax(jnp.max(scores, axis=0), 'row')  248 us
    psum x1, waiting for transfers between devices, per_device(): moment = lax.psum(partial_moment, ('row', 'col'))  234 us
    pmax x3, blocking collectives, row_totals(): top_score = lax.pmax(jnp.max(scores, axis=1), 'col')  46.5 us
    psum x3, blocking collectives, row_totals(): lax.psum(jnp.sum(jnp.exp(scores - top_score[:, None]), axis=1), 'col')  46.2 us
    all_gather x2, blocking collectives, column_totals(): lax.all_gather(jnp.sum(jnp.exp(scores - top_score[None, :]), axis=0), 'row')  43.5 us
    all_gather x1, blocking collectives, per_device(): rows_block = lax.all_gather(source, 'col', axis=0, tiled=True)  27.7 us
    reduce_sum x3, other arithmetic, row_totals(): jnp.sum(jnp.exp(scores - top_score[:, None]), axis=1)  23.5 us
    all_gather x1, blocking collectives, per_device(): lax.all_gather(target_potential, 'row', axis=0, tiled=True)  21.8 us
  transfers between devices with their start and end apart: 2, of which 2 were waited for; matrix products, arithmetic and copies ran while one was open for 0% of the time, Pallas kernels for 0%

profile of v1, /device:TPU:32, one launch (start us, length us, event | category | flops | bytes accessed | tf_op | source)
XLA Modules:
  0.0 775.5 jit_solution(6265074148045334683)
XLA Ops:
  7.2 0.0 copy-start
  7.2 0.0 all-gather.5.cloned.1.call-start
  7.2 0.7 all-gather.5.cloned.1.call-update
  7.9 0.0 all-reduce.2.cloned.1.call-start
  8.0 21.8 %all-gather.2 = bf16[32,1,128]{2,1,0:T(2,128)(2,1)S(1)} all-gather(bf16[1,1,128]{2,1,0:T(2,128)(2,1)} %bitcast.20), channel_id=1, replica_groups=mesh['row'=32,'col'=8] {'row'}, dimensions={0}, use_global_device_ids=true | all-gather | bytes 8448 | tf_op jit(solution)/shard_map/all_gather | solution.py:40
  29.8 27.7 %all_gather.22 = bf16[1024,128]{1,0:T(8,128)(2,1)S(1)} all-gather(bf16[128,128]{1,0:T(8,128)(2,1)} %param.4), channel_id=1, replica_groups=mesh['row'=32,'col'=8] {'col'}, dimensions={0}, use_global_device_ids=true | all-gather | bytes 294912 | tf_op jit(solution)/shard_map/all_gather | solution.py:37
  57.5 0.0 copy-done
  57.5 0.4 convolution_convert_fusion.1
  57.9 3.1 all-gather.5.cloned.1.call-done
  61.0 0.0 copy-start.1
  61.0 8.3 %fusion = (f32[1024]{0:T(1024)S(1)}, f32[1024,4096]{1,0:T(8,128)}) fusion(f32[4096]{0:T(1024)S(1)} %bitcast.15, bf16[1024,128]{1,0:T(8,128)(2,1)S(1)} %convolution_convert_fusion.1, bf16[4096,128]{1,0:T(8,128)(2,1)} %all-gather.5.cloned.1.call-done), kind=kOutput, calls=%fused_computation.11 | convolution fusion | flops 1086323712 | bytes 18108416 | tf_op jit(solution)/shard_map/dot_general | solution.py:17
  69.3 16.0 %pmax.35 = f32[1024]{0:T(1024)S(1)} all-reduce(f32[1024]{0:T(1024)S(1)} %get-tuple-element.12), channel_id=1, replica_groups=mesh['row'=32,'col'=8] {'col'}, use_global_device_ids=true, to_apply=%region_1.0 | all-reduce | flops 1024 | bytes 8192 | tf_op jit(solution)/shard_map/pmax | solution.py:23
  85.4 7.8 %exponential_reduce_fusion.4 = f32[1024]{0:T(1024)S(1)} fusion(f32[1024,4096]{1,0:T(8,128)} %get-tuple-element.13, f32[1024]{0:T(1024)S(1)} %pmax.35, f32[4096]{0:T(1024)S(1)} %bitcast.16), kind=kLoop, calls=%fused_computation.5 | loop fusion | flops 16776192 | bytes 16801792 | tf_op jit(solution)/shard_map/reduce_sum | solution.py:24
  93.2 16.0 %psum.28 = f32[1024]{0:T(1024)S(1)} all-reduce(f32[1024]{0:T(1024)S(1)} %exponential_reduce_fusion.4), channel_id=1, replica_groups=mesh['row'=32,'col'=8] {'col'}, use_global_device_ids=true, to_apply=%region_3.0 | all-reduce | flops 1024 | bytes 8192 | tf_op jit(solution)/shard_map/psum | solution.py:24
  109.2 0.0 copy-done.1
  109.2 7.8 %fusion.1 = f32[1024,128]{1,0:T(8,128)S(1)} fusion(bf16[4096,128]{1,0:T(8,128)(2,1)S(1)} %copy-done.1, f32[1024,4096]{1,0:T(8,128)} %get-tuple-element.13, f32[1024]{0:T(1024)S(1)} %log_add_fusion, f32[4096]{0:T(1024)S(1)} %bitcast.17), kind=kOutput, calls=%fused_computation.12 | convolution fusion | flops 1094713344 | bytes 18370560 | tf_op jit(solution)/shard_map/dot_general | solution.py:51
  117.0 1.2 convolution_bitcast_fusion
  118.2 0.0 all-reduce.2.cloned.1.call-update
  118.3 234.4 %all-reduce.2.cloned.1.call-done = f32[128,128]{0,1:T(8,128)} async-done(((f32[128,128]{0,1:T(8,128)}), f32[128,128]{0,1:T(8,128)}) %all-reduce.2.cloned.1.call-update) | async-done | bytes 65552 | tf_op jit(solution)/shard_map/psum | solution.py:58
  352.7 1.2 convolution_convert_fusion
  353.9 7.0 subtract_reduce_fusion.3
  360.9 15.2 %pmax.36 = f32[1024]{0:T(1024)S(1)} all-reduce(f32[1024]{0:T(1024)S(1)} %get-tuple-element.14), channel_id=1, replica_groups=mesh['row'=32,'col'=8] {'col'}, use_global_device_ids=true, to_apply=%region_6.0 | all-reduce | flops 1024 | bytes 8192 | tf_op jit(solution)/shard_map/pmax | solution.py:23
  376.1 7.8 %exponential_reduce_fusion.3 = f32[1024]{0:T(1024)S(1)} fusion(f32[1024,4096]{1,0:T(8,128)} %get-tuple-element.15, f32[1024]{0:T(1024)S(1)} %pmax.36, f32[4096]{0:T(1024)S(1)} %bitcast.19), kind=kLoop, calls=%fused_computation.3 | loop fusion | flops 16776192 | bytes 16801792 | tf_op jit(solution)/shard_map/reduce_sum | solution.py:24
  384.0 15.1 %psum.30 = f32[1024]{0:T(1024)S(1)} all-reduce(f32[1024]{0:T(1024)S(1)} %exponential_reduce_fusion.3), channel_id=1, replica_groups=mesh['row'=32,'col'=8] {'col'}, use_global_device_ids=true, to_apply=%region_8.0 | all-reduce | flops 1024 | bytes 8192 | tf_op jit(solution)/shard_map/psum | solution.py:24
  399.1 7.7 subtract_reduce_fusion.2
  406.8 124.0 %pmax.37 = f32[4096]{0:T(1024)S(1)} all-reduce(f32[4096]{0:T(1024)S(1)} %subtract_reduce_fusion.2), channel_id=1, replica_groups=mesh['row'=32,'col'=8] {'row'}, use_global_device_ids=true, to_apply=%region_10.0 | all-reduce | flops 4096 | bytes 32768 | tf_op jit(solution)/shard_map/pmax | solution.py:29
  530.8 7.7 exponential_reduce_fusion.2
  538.5 21.8 %all-gather = f32[131072]{0:T(1024)S(1)} all-gather(f32[4096]{0:T(1024)S(1)} %exponential_reduce_fusion.2), channel_id=2, replica_groups=mesh['row'=32,'col'=8] {'row'}, dimensions={0}, use_global_device_ids=true | all-gather | bytes 540672 | tf_op jit(solution)/shard_map/all_gather | solution.py:31
  560.3 0.1 reshape.16
  560.4 0.1 reduce_sum.66
  560.5 7.5 subtract_reduce_fusion.1
  567.9 15.2 %pmax.38 = f32[1024]{0:T(1024)S(1)} all-reduce(f32[1024]{0:T(1024)S(1)} %subtract_reduce_fusion.1), channel_id=1, replica_groups=mesh['row'=32,'col'=8] {'col'}, use_global_device_ids=true, to_apply=%region_14.0 | all-reduce | flops 1024 | bytes 8192 | tf_op jit(solution)/shard_map/pmax | solution.py:23
  583.2 7.8 %exponential_reduce_fusion.1 = f32[1024]{0:T(1024)S(1)} fusion(f32[1024,4096]{1,0:T(8,128)} %get-tuple-element.15, f32[1024]{0:T(1024)S(1)} %pmax.38, f32[4096]{0:T(1024)S(1)} %add_subtract_fusion), kind=kLoop, calls=%fused_computation.1 | loop fusion | flops 16776192 | bytes 16801792 | tf_op jit(solution)/shard_map/reduce_sum | solution.py:24
  591.0 15.1 %psum.31 = f32[1024]{0:T(1024)S(1)} all-reduce(f32[1024]{0:T(1024)S(1)} %exponential_reduce_fusion.1), channel_id=1, replica_groups=mesh['row'=32,'col'=8] {'col'}, use_global_device_ids=true, to_apply=%region_16.0 | all-reduce | flops 1024 | bytes 8192 | tf_op jit(solution)/shard_map/psum | solution.py:24
  606.1 0.0 copy-start.3
  606.1 0.0 copy-start.2
  606.1 7.8 %subtract_reduce_fusion = f32[4096]{0:T(1024)S(1)} fusion(f32[1024,4096]{1,0:T(8,128)} %get-tuple-element.15, f32[1024]{0:T(1024)S(1)} %add_subtract_fusion.1), kind=kLoop, calls=%fused_computation.7 | loop fusion | flops 12578816 | bytes 16797696 | tf_op jit(solution)/shard_map/reduce_max | solution.py:29
  613.9 123.8 %pmax.39 = f32[4096]{0:T(1024)S(1)} all-reduce(f32[4096]{0:T(1024)S(1)} %subtract_reduce_fusion), channel_id=1, replica_groups=mesh['row'=32,'col'=8] {'row'}, use_global_device_ids=true, to_apply=%region_18.0 | all-reduce | flops 4096 | bytes 32768 | tf_op jit(solution)/shard_map/pmax | solution.py:29
  737.7 7.7 exponential_reduce_fusion
  745.4 0.0 copy-done.3
  745.4 21.8 %all-gather.1 = f32[131072]{0:T(1024)S(1)} all-gather(f32[4096]{0:T(1024)S(1)} %exponential_reduce_fusion), channel_id=3, replica_groups=mesh['row'=32,'col'=8] {'row'}, dimensions={0}, use_global_device_ids=true | all-gather | bytes 540672 | tf_op jit(solution)/shard_map/all_gather | solution.py:31
  767.2 0.1 reshape.17
  767.3 0.1 reduce_sum.69
  767.3 0.6 fusion.2
  767.9 0.0 copy-done.2
  767.9 0.7 copy.9
  (5 shorter events, 0.1 us)
Async XLA Ops:
  7.2 50.3 %copy-start = (f32[128,128]{1,0:T(8,128)S(1)}, f32[128,128]{1,0:T(8,128)}, u32[]{:S(2)}) copy-start(f32[128,128]{1,0:T(8,128)} %param.7) | copy-start | bytes 196612
  7.2 53.8 %all-gather.5.cloned.1.call-start = ((), (), s32[]{:S(2)}) async-start(), calls=%async_computation | async-start | bytes 1081344 | tf_op jit(solution)/shard_map/all_gather | solution.py:39
  7.9 344.7 %all-reduce.2.cloned.1.call-start = ((), (), s32[]{:S(2)}) async-start(), calls=%async_computation.1 | async-start | bytes 131072 | tf_op jit(solution)/shard_map/psum | solution.py:58
  61.0 48.2 %copy-start.1 = (bf16[4096,128]{1,0:T(8,128)(2,1)S(1)}, bf16[4096,128]{1,0:T(8,128)(2,1)}, u32[]{:S(2)}) copy-start(bf16[4096,128]{1,0:T(8,128)(2,1)} %all-gather.5.cloned.1.call-done) | copy-start | bytes 3145732
  606.1 139.3 %copy-start.3 = (f32[1024]{0:T(1024)}, f32[1024]{0:T(1024)S(1)}, u32[]{:S(2)}) copy-start(f32[1024]{0:T(1024)S(1)} %add_subtract_fusion.1) | copy-start | bytes 12292
  606.1 161.8 %copy-start.2 = (f32[128,128]{0,1:T(8,128)S(1)}, f32[128,128]{0,1:T(8,128)}, u32[]{:S(2)}) copy-start(f32[128,128]{0,1:T(8,128)} %all-reduce.2.cloned.1.call-done) | copy-start | bytes 196612
Sparse Core Ops, SparseCore 0:
  10.6 50.3 all-gather.4
  118.4 234.2 all-reduce.1
